TPU v7x, 32 devices: a whole 2x2x4 slice. The times are simulated.
32 devices in a mesh: seq: 16 (over z, x, core), tp: 2 (over y).
Axes of the slice: x: 2, y: 2, z: 4, core: 2. Of those that a mesh axis runs over, the one named last changes fastest.
Arguments:
- frames: bfloat16 [2, 4, 1024, 1024], P(None, 'tp', 'seq'), may hold values from -6 to 6
- time_embed: float32 [2, 4, 1024], replicated, may hold values from -6 to 6
- lengths: int32 [2, 4], replicated, may hold values from 1 to 1024, 2560 in all within a row
- w_query: bfloat16 [1024, 1024], P('seq', 'tp'), may hold values from -0.1875 to 0.1875
- w_key: bfloat16 [1024, 1024], P('seq', 'tp'), may hold values from -0.1875 to 0.1875
- w_value: bfloat16 [1024, 1024], P('seq', 'tp'), may hold values from -0.1875 to 0.1875
- w_out: bfloat16 [1024, 1024], P('tp', 'seq'), may hold values from -0.75 to 0.75
- w_up: bfloat16 [1024, 2048], P('seq', 'tp'), may hold values from -0.1875 to 0.1875
- w_down: bfloat16 [2048, 1024], P('tp', 'seq'), may hold values from -0.125 to 0.125
- w_mod: bfloat16 [1024, 6144], P('seq', 'tp'), may hold values from -0.1875 to 0.1875
- out_grad: bfloat16 [2, 4, 1024, 1024], P(None, 'tp', 'seq'), may hold values from -6 to 6
Outputs:
- layer_out: bfloat16 [2, 4, 1024, 1024], P(None, 'tp', 'seq')
- grad_input: bfloat16 [2, 4, 1024, 1024], P(None, 'tp', 'seq')
- grad_query: float32 [1024, 1024], P('seq', 'tp')
- grad_key: float32 [1024, 1024], P('seq', 'tp')
- grad_value: float32 [1024, 1024], P('seq', 'tp')
- grad_out: float32 [1024, 1024], P('tp', 'seq')
- grad_up: float32 [1024, 2048], P('seq', 'tp')
- grad_down: float32 [2048, 1024], P('tp', 'seq')
- grad_mod: float32 [1024, 6144], P('seq', 'tp')
Inputs may be any that keep to these rules, and one draw needn't show every extreme that they name: In every micro-batch the 4 lengths add up to 2560, and one item has exactly 1024 live frames.
All inputs are finite; a program needn't handle non-finite values.
Results may differ from a plain program's by a relative error of at most 0.024.
Values may be sent and summed in bfloat16 or wider, within the bound.
A program may use at most 384 MiB of HBM per device.

v0:
```python
from functools import partial
import math

import jax
import jax.numpy as jnp
from jax import lax
from jax.sharding import PartitionSpec as P

D = 1024
HEAD_DIM = 64


EPSILON = 1e-06
HIGHEST = lax.Precision.HIGHEST
NEGATIVE = -1e30


def layer_stats(values):
    center = values - jnp.mean(values, axis=-1, keepdims=True)
    inverse = lax.rsqrt(jnp.mean(center * center, axis=-1, keepdims=True) + EPSILON)
    return (center * inverse, inverse)


def layer_back(normed, inverse, incoming):
    return inverse * (
        incoming
        - jnp.mean(incoming, axis=-1, keepdims=True)
        - normed * jnp.mean(incoming * normed, axis=-1, keepdims=True)
    )


def rotary_tables(first_row, row_count, column_count, head_size):
    position = (first_row + jnp.arange(row_count)).astype(jnp.float32)
    column = (jnp.arange(column_count) % head_size // 2).astype(jnp.float32)
    inverse = jnp.exp(column * (-2.0 * math.log(10000.0) / head_size))
    angles = position[:, None] * inverse[None, :]
    return (jnp.cos(angles), jnp.sin(angles))


def turn_half(values):
    paired = values.reshape(values.shape[:-1] + (values.shape[-1] // 2, 2))
    return jnp.stack((-paired[..., 1], paired[..., 0]), axis=-1).reshape(values.shape)


def reduce_grads(gradients):
    return (
        lax.psum_scatter(
            gradients[0].astype(jnp.bfloat16), "seq", scatter_dimension=0, tiled=True
        ).astype(jnp.float32),
        lax.psum_scatter(
            gradients[1].astype(jnp.bfloat16), "seq", scatter_dimension=0, tiled=True
        ).astype(jnp.float32),
        lax.psum_scatter(
            gradients[2].astype(jnp.bfloat16), "seq", scatter_dimension=0, tiled=True
        ).astype(jnp.float32),
        lax.psum_scatter(
            gradients[3].astype(jnp.bfloat16), "seq", scatter_dimension=1, tiled=True
        ).astype(jnp.float32),
        lax.psum_scatter(
            gradients[4].astype(jnp.bfloat16), "seq", scatter_dimension=0, tiled=True
        ).astype(jnp.float32),
        lax.psum_scatter(
            gradients[5].astype(jnp.bfloat16), "seq", scatter_dimension=1, tiled=True
        ).astype(jnp.float32),
        lax.psum_scatter(
            gradients[6].astype(jnp.bfloat16), "seq", scatter_dimension=0, tiled=True
        ).astype(jnp.float32),
    )


def per_device(
    frames, time_embed, lengths, w_query, w_key, w_value, w_out, w_up, w_down, w_mod, out_grad
):
    micro_count = frames.shape[0]
    rows_own = frames.shape[1]
    frames_local = frames.shape[2]
    batch_items = lengths.shape[1]
    frames_total = frames_local * lax.axis_size("seq")
    own_index = lax.axis_index("tp")
    sequence_start = lax.axis_index("seq") * frames_local
    head_cols = w_query.shape[1]
    local_heads = head_cols // HEAD_DIM
    factor = HEAD_DIM ** (-0.5)
    cosine, sine_table = rotary_tables(sequence_start, frames_local, head_cols, HEAD_DIM)
    position = sequence_start + jnp.arange(frames_local)
    key_position = jnp.arange(frames_total)

    def to_heads(tensor):
        return tensor.reshape(tensor.shape[:2] + (local_heads, HEAD_DIM))

    outputs = []
    input_grads = []
    totals = None
    for batch_index in range(micro_count):
        query_full, key_full, value_full, out_full, up_full, down_full, mod_full = (
            lax.all_gather(w_query, "seq", axis=0, tiled=True),
            lax.all_gather(w_key, "seq", axis=0, tiled=True),
            lax.all_gather(w_value, "seq", axis=0, tiled=True),
            lax.all_gather(w_out, "seq", axis=1, tiled=True),
            lax.all_gather(w_up, "seq", axis=0, tiled=True),
            lax.all_gather(w_down, "seq", axis=1, tiled=True),
            lax.all_gather(w_mod, "seq", axis=0, tiled=True),
        )
        silu_time = jax.nn.silu(time_embed[batch_index]).astype(jnp.bfloat16)
        mod_block = jnp.dot(silu_time, mod_full, preferred_element_type=jnp.float32).astype(
            jnp.bfloat16
        )
        frame_rows = frames[batch_index].astype(jnp.float32)
        normed_a, inverse_a = layer_stats(frame_rows)
        normed_all, mod_all = (
            lax.all_gather(normed_a.astype(jnp.bfloat16), "tp", axis=0, tiled=True),
            lax.all_gather(mod_block, "tp", axis=1, tiled=True),
        )
        modulation = mod_all.astype(jnp.float32)
        shift_attn = modulation[:, 0:D]
        scale_attn = modulation[:, D : 2 * D]
        gate_attn = modulation[:, 2 * D : 3 * D]
        shift_ff = modulation[:, 3 * D : 4 * D]
        scale_ff = modulation[:, 4 * D : 5 * D]
        gate_ff = modulation[:, 5 * D : 6 * D]
        item_lengths = lengths[batch_index]
        own_lengths = lax.dynamic_slice_in_dim(item_lengths, own_index * rows_own, rows_own, 0)
        live_rows = (position[None, :] < own_lengths[:, None]).astype(jnp.float32)
        key_live = key_position[None, :] < item_lengths[:, None]
        gate_attn_own = lax.dynamic_slice_in_dim(gate_attn, own_index * rows_own, rows_own, 0)
        gate_ff_own = lax.dynamic_slice_in_dim(gate_ff, own_index * rows_own, rows_own, 0)
        normed_a_wide = normed_all.astype(jnp.float32)
        modulated_a = (
            normed_a_wide * (1.0 + scale_attn[:, None, :]) + shift_attn[:, None, :]
        ).astype(jnp.bfloat16)
        query_lin = jnp.einsum(
            "bld,dc->blc", modulated_a, query_full, preferred_element_type=jnp.float32
        )
        key_lin = jnp.einsum(
            "bld,dc->blc", modulated_a, key_full, preferred_element_type=jnp.float32
        )
        value_rows = jnp.einsum(
            "bld,dc->blc", modulated_a, value_full, preferred_element_type=jnp.float32
        ).astype(jnp.bfloat16)
        queries = (query_lin * cosine + turn_half(query_lin) * sine_table).astype(jnp.bfloat16)
        key_rows = (key_lin * cosine + turn_half(key_lin) * sine_table).astype(jnp.bfloat16)
        keys_all, values_all = (
            lax.all_gather(key_rows, "seq", axis=1, tiled=True),
            lax.all_gather(value_rows, "seq", axis=1, tiled=True),
        )
        query_heads = to_heads(queries)
        key_heads = to_heads(keys_all)
        value_heads = to_heads(values_all)

        def masked_scores():
            scores = (
                jnp.einsum(
                    "bqhd,bkhd->bhqk", query_heads, key_heads, preferred_element_type=jnp.float32
                )
                * factor
            )
            return jnp.where(key_live[:, None, None, :], scores, NEGATIVE)

        scores = masked_scores()
        highest = jnp.max(scores, axis=-1, keepdims=True)
        unnormed = jnp.exp(scores - highest)
        row_total = jnp.sum(unnormed, axis=-1, keepdims=True)
        softmax_rows = unnormed / row_total
        log_total = highest + jnp.log(row_total)
        attended = (
            jnp.einsum(
                "bhqk,bkhd->bqhd",
                softmax_rows.astype(jnp.bfloat16),
                value_heads,
                preferred_element_type=jnp.float32,
            )
            .reshape(batch_items, frames_local, head_cols)
            .astype(jnp.bfloat16)
        )
        branch_a = lax.psum_scatter(
            jnp.einsum(
                "blc,cd->bld", attended, out_full, preferred_element_type=jnp.float32
            ).astype(jnp.bfloat16),
            "tp",
            scatter_dimension=0,
            tiled=True,
        ).astype(jnp.float32)
        middle = frame_rows + gate_attn_own[:, None, :] * live_rows[:, :, None] * branch_a
        normed_f, inverse_f = layer_stats(middle)
        normed_f_all = lax.all_gather(normed_f.astype(jnp.bfloat16), "tp", axis=0, tiled=True)
        normed_f_wide = normed_f_all.astype(jnp.float32)
        modulated_f = (normed_f_wide * (1.0 + scale_ff[:, None, :]) + shift_ff[:, None, :]).astype(
            jnp.bfloat16
        )
        upper = jnp.einsum("bld,df->blf", modulated_f, up_full, preferred_element_type=jnp.float32)
        active, gelu_back = jax.vjp(partial(jax.nn.gelu, approximate=True), upper)
        active = active.astype(jnp.bfloat16)
        project_block = lax.slice_in_dim(active, 0, rows_own * lax.axis_size("tp"), axis=0)
        branch_f = lax.psum_scatter(
            jnp.einsum(
                "blf,fd->bld", project_block, down_full, preferred_element_type=jnp.float32
            ).astype(jnp.bfloat16),
            "tp",
            scatter_dimension=0,
            tiled=True,
        ).astype(jnp.float32)
        outputs.append((middle + gate_ff_own[:, None, :] * branch_f).astype(jnp.bfloat16))
        cotangent = out_grad[batch_index].astype(jnp.float32)
        delta_gate_ff = jnp.sum(cotangent * branch_f, axis=1)
        delta_branch_f = (cotangent * gate_ff_own[:, None, :]).astype(jnp.bfloat16)
        branch_f_all = lax.all_gather(delta_branch_f, "tp", axis=0, tiled=True)
        delta_active = jnp.einsum(
            "bld,fd->blf", branch_f_all, down_full, preferred_element_type=jnp.float32
        )
        delta_upper = gelu_back(delta_active)[0].astype(jnp.bfloat16)
        grad_down = jnp.einsum(
            "blf,bld->fd", active, branch_f_all, preferred_element_type=jnp.float32
        )
        grad_up = jnp.einsum(
            "bld,blf->df", modulated_f, delta_upper, preferred_element_type=jnp.float32
        )
        delta_mod_f = jnp.einsum(
            "blf,df->bld", delta_upper, up_full, preferred_element_type=jnp.float32
        )
        delta_shift_ff = jnp.sum(delta_mod_f, axis=1)
        delta_scale_ff = jnp.sum(delta_mod_f * normed_f_wide, axis=1)
        delta_norm_f = delta_mod_f * (1.0 + scale_ff[:, None, :])
        norm_f_own = lax.psum_scatter(
            delta_norm_f.astype(jnp.bfloat16), "tp", scatter_dimension=0, tiled=True
        ).astype(jnp.float32)
        delta_middle = cotangent + layer_back(normed_f, inverse_f, norm_f_own)
        delta_gate_attn = jnp.sum(delta_middle * live_rows[:, :, None] * branch_a, axis=1)
        delta_branch_a = (delta_middle * gate_attn_own[:, None, :] * live_rows[:, :, None]).astype(
            jnp.bfloat16
        )
        branch_a_all = lax.all_gather(delta_branch_a, "tp", axis=0, tiled=True)
        grad_out = jnp.einsum(
            "blc,bld->cd", attended, branch_a_all, preferred_element_type=jnp.float32
        )
        delta_attended = jnp.einsum(
            "bld,cd->blc", branch_a_all, out_full, preferred_element_type=jnp.float32
        ).astype(jnp.bfloat16)
        attend_heads = to_heads(delta_attended)
        softmax_again = jnp.exp(masked_scores() - log_total)
        delta_probs = jnp.einsum(
            "bqhd,bkhd->bhqk", attend_heads, value_heads, preferred_element_type=jnp.float32
        )
        row_dot = jnp.sum(softmax_again * delta_probs, axis=-1, keepdims=True)
        delta_scores = (softmax_again * (delta_probs - row_dot)).astype(jnp.bfloat16)
        delta_queries = (
            jnp.einsum(
                "bhqk,bkhd->bqhd", delta_scores, key_heads, preferred_element_type=jnp.float32
            )
            * factor
        ).reshape(batch_items, frames_local, head_cols)
        part_keys = (
            jnp.einsum(
                "bhqk,bqhd->bkhd", delta_scores, query_heads, preferred_element_type=jnp.float32
            )
            * factor
        )
        part_values = jnp.einsum(
            "bhqk,bqhd->bkhd",
            softmax_again.astype(jnp.bfloat16),
            attend_heads,
            preferred_element_type=jnp.float32,
        )
        delta_keys, delta_values = (
            lax.psum_scatter(
                part_keys.reshape(batch_items, frames_total, head_cols).astype(jnp.bfloat16),
                "seq",
                scatter_dimension=1,
                tiled=True,
            ).astype(jnp.float32),
            lax.psum_scatter(
                part_values.reshape(batch_items, frames_total, head_cols).astype(jnp.bfloat16),
                "seq",
                scatter_dimension=1,
                tiled=True,
            ).astype(jnp.float32),
        )
        delta_query_lin = (delta_queries * cosine - turn_half(delta_queries) * sine_table).astype(
            jnp.bfloat16
        )
        delta_key_lin = (delta_keys * cosine - turn_half(delta_keys) * sine_table).astype(
            jnp.bfloat16
        )
        delta_value_lin = delta_values.astype(jnp.bfloat16)
        grad_query = jnp.einsum(
            "bld,blc->dc", modulated_a, delta_query_lin, preferred_element_type=jnp.float32
        )
        grad_key = jnp.einsum(
            "bld,blc->dc", modulated_a, delta_key_lin, preferred_element_type=jnp.float32
        )
        grad_value = jnp.einsum(
            "bld,blc->dc", modulated_a, delta_value_lin, preferred_element_type=jnp.float32
        )
        delta_mod_a = (
            jnp.einsum(
                "blc,dc->bld", delta_query_lin, query_full, preferred_element_type=jnp.float32
            )
            + jnp.einsum("blc,dc->bld", delta_key_lin, key_full, preferred_element_type=jnp.float32)
            + jnp.einsum(
                "blc,dc->bld", delta_value_lin, value_full, preferred_element_type=jnp.float32
            )
        )
        delta_norm_a = delta_mod_a * (1.0 + scale_attn[:, None, :])
        empty_rows = jnp.zeros((batch_items, D), jnp.float32)
        gate_attn_rows = lax.dynamic_update_slice_in_dim(
            empty_rows, delta_gate_attn, own_index * rows_own, 0
        )
        gate_ff_rows = lax.dynamic_update_slice_in_dim(
            empty_rows, delta_gate_ff, own_index * rows_own, 0
        )
        delta_modulation = jnp.concatenate(
            [
                jnp.sum(delta_mod_a, axis=1),
                jnp.sum(delta_mod_a * normed_a_wide, axis=1),
                gate_attn_rows,
                delta_shift_ff,
                delta_scale_ff,
                gate_ff_rows,
            ],
            axis=1,
        )
        norm_a_own, mod_grad_block = (
            lax.psum_scatter(
                delta_norm_a.astype(jnp.bfloat16), "tp", scatter_dimension=0, tiled=True
            ).astype(jnp.float32),
            lax.psum_scatter(
                delta_modulation.astype(jnp.bfloat16), "tp", scatter_dimension=1, tiled=True
            ).astype(jnp.float32),
        )
        input_grads.append(
            (delta_middle + layer_back(normed_a, inverse_a, norm_a_own)).astype(jnp.bfloat16)
        )
        grad_mod = jnp.dot(silu_time.astype(jnp.float32).T, mod_grad_block, precision=HIGHEST)
        gradients = (grad_query, grad_key, grad_value, grad_out, grad_up, grad_down, grad_mod)
        gradients = reduce_grads(gradients)
        if totals is None:
            totals = gradients
        else:
            totals = tuple((earlier + later for earlier, later in zip(totals, gradients)))
    return (
        jnp.stack(outputs),
        jnp.stack(input_grads),
        totals[0],
        totals[1],
        totals[2],
        totals[3],
        totals[4],
        totals[5],
        totals[6],
    )


def solution(mesh):
    return jax.shard_map(
        per_device,
        mesh=mesh,
        in_specs=(
            P(None, "tp", "seq", None),
            P(),
            P(),
            P("seq", "tp"),
            P("seq", "tp"),
            P("seq", "tp"),
            P("tp", "seq"),
            P("seq", "tp"),
            P("tp", "seq"),
            P("seq", "tp"),
            P(None, "tp", "seq", None),
        ),
        out_specs=(
            P(None, "tp", "seq", None),
            P(None, "tp", "seq", None),
            P("seq", "tp"),
            P("seq", "tp"),
            P("seq", "tp"),
            P("tp", "seq"),
            P("seq", "tp"),
            P("tp", "seq"),
            P("seq", "tp"),
        ),
        check_vma=False,
    )
```

profile of v0, /device:TPU:0, one launch (start us, length us, event | category | flops | bytes accessed | tf_op | source)
XLA Modules:
  0.0 2039.6 jit_solution(13790267444647037653)
XLA Ops:
  13.6 9.9 all_gather.83
  24.1 50.8 %all-gather.12.cloned.1.call-done = bf16[1024,3072]{1,0:T(8,128)(2,1)} async-done(((bf16[64,3072]{1,0:T(8,128)(2,1)}), bf16[1024,3072]{1,0:T(8,128)(2,1)}) %all-gather.12.cloned.1.call-update) | async-done | bytes 6291472 | tf_op jit(solution)/shard_map/all_gather | solution.py:102
  84.3 29.3 %all-gather.20.cloned.1.call-done = bf16[1024,512]{1,0:T(8,128)(2,1)} async-done(((bf16[64,512]{1,0:T(8,128)(2,1)}), bf16[1024,512]{1,0:T(8,128)(2,1)}) %all-gather.20.cloned.1.call-update) | async-done | bytes 1048592 | tf_op jit(solution)/shard_map/all_gather | solution.py:97
  117.9 34.7 %all-gather.18.cloned.1.call-done = bf16[1024,512]{1,0:T(8,128)(2,1)} async-done(((bf16[64,512]{1,0:T(8,128)(2,1)}), bf16[1024,512]{1,0:T(8,128)(2,1)}) %all-gather.18.cloned.1.call-update) | async-done | bytes 1048592 | tf_op jit(solution)/shard_map/all_gather | solution.py:96
  158.0 33.5 %all-gather.14.cloned.1.call-done = bf16[1024,512]{1,0:T(8,128)(2,1)} async-done(((bf16[64,512]{1,0:T(8,128)(2,1)}), bf16[1024,512]{1,0:T(8,128)(2,1)}) %all-gather.14.cloned.1.call-update) | async-done | bytes 1048592 | tf_op jit(solution)/shard_map/all_gather | solution.py:98
  195.8 47.9 %all-gather.32.cloned.1.call-done = bf16[4,1024,512]{2,1,0:T(8,128)(2,1)} async-done(((bf16[4,64,512]{2,1,0:T(8,128)(2,1)}), bf16[4,1024,512]{2,1,0:T(8,128)(2,1)}) %all-gather.32.cloned.1.call-update) | async-done | bytes 4194320 | tf_op jit(solution)/shard_map/all_gather | solution.py:143
  250.0 7.0 fusion.13
  257.0 38.4 %all-gather.30.cloned.1.call-done = bf16[4,1024,512]{2,1,0:T(8,128)(2,1)} async-done(((bf16[4,64,512]{2,1,0:T(8,128)(2,1)}), bf16[4,1024,512]{2,1,0:T(8,128)(2,1)}) %all-gather.30.cloned.1.call-update) | async-done | bytes 4194320 | tf_op jit(solution)/shard_map/all_gather | solution.py:144
  311.5 22.6 %all-gather.24.cloned.1.call-done = bf16[512,1024]{0,1:T(8,128)(2,1)} async-done(((bf16[512,64]{0,1:T(8,128)(2,1)}), bf16[512,1024]{0,1:T(8,128)(2,1)}) %all-gather.24.cloned.1.call-update) | async-done | bytes 1048592 | tf_op jit(solution)/shard_map/all_gather | solution.py:99
  355.7 8.9 all_gather.72
  388.2 7.9 all_gather.89
  397.5 7.4 all_gather.86
  408.4 28.9 %all-gather.28.cloned.1.call-done = bf16[1024,1024]{0,1:T(8,128)(2,1)} async-done(((bf16[1024,64]{0,1:T(8,128)(2,1)}), bf16[1024,1024]{0,1:T(8,128)(2,1)}) %all-gather.28.cloned.1.call-update) | async-done | bytes 2097168 | tf_op jit(solution)/shard_map/all_gather | solution.py:101
  443.1 46.0 %all-gather.22.cloned.1.call-done = bf16[4,1024,512]{2,1,0:T(8,128)(2,1)} async-done(((bf16[4,64,512]{2,1,0:T(8,128)(2,1)}), bf16[4,1024,512]{2,1,0:T(8,128)(2,1)}) %all-gather.22.cloned.1.call-update) | async-done | bytes 4194320 | tf_op jit(solution)/shard_map/all_gather | solution.py:143
  505.0 36.0 %all-gather.16.cloned.1.call-done = bf16[4,1024,512]{2,1,0:T(8,128)(2,1)} async-done(((bf16[4,64,512]{2,1,0:T(8,128)(2,1)}), bf16[4,1024,512]{2,1,0:T(8,128)(2,1)}) %all-gather.16.cloned.1.call-update) | async-done | bytes 4194320 | tf_op jit(solution)/shard_map/all_gather | solution.py:144
  547.3 7.6 fusion.43
  558.8 15.0 reduce-scatter.33.cloned.1.call-done
  577.9 9.1 all_gather.90
  590.2 7.9 multiply_reduce_fusion
  614.2 7.9 fusion.17
  638.0 48.9 %reduce-scatter.51.cloned.1.call-done = bf16[4,64,512]{2,1,0:T(8,128)(2,1)} async-done(((bf16[4,1024,512]{2,1,0:T(8,128)(2,1)}), bf16[4,64,512]{2,1,0:T(8,128)(2,1)}) %reduce-scatter.51.cloned.1.call-update) | async-done | bytes 262160 | tf_op jit(solution)/shard_map/reduce_scatter | solution.py:264
  697.6 64.6 %reduce-scatter.53.cloned.1.call-done = bf16[4,64,512]{2,1,0:T(8,128)(2,1)} async-done(((bf16[4,1024,512]{2,1,0:T(8,128)(2,1)}), bf16[4,64,512]{2,1,0:T(8,128)(2,1)}) %reduce-scatter.53.cloned.1.call-update) | async-done | bytes 262160 | tf_op jit(solution)/shard_map/reduce_scatter | solution.py:270
  765.8 15.1 all_gather.87
  785.3 9.1 all_gather.79
  805.1 8.9 reduce-scatter.41.cloned.1.call-done
  814.1 17.5 reduce-scatter.35.cloned.1.call-done
  836.4 8.7 all_gather.88
  848.3 7.9 multiply_reduce_fusion.1
  872.3 8.0 fusion.14
  899.9 44.9 %reduce-scatter.43.cloned.1.call-done = bf16[4,64,512]{2,1,0:T(8,128)(2,1)} async-done(((bf16[4,1024,512]{2,1,0:T(8,128)(2,1)}), bf16[4,64,512]{2,1,0:T(8,128)(2,1)}) %reduce-scatter.43.cloned.1.call-update) | async-done | bytes 262160 | tf_op jit(solution)/shard_map/reduce_scatter | solution.py:264
  956.7 64.0 %reduce-scatter.45.cloned.1.call-done = bf16[4,64,512]{2,1,0:T(8,128)(2,1)} async-done(((bf16[4,1024,512]{2,1,0:T(8,128)(2,1)}), bf16[4,64,512]{2,1,0:T(8,128)(2,1)}) %reduce-scatter.45.cloned.1.call-update) | async-done | bytes 262160 | tf_op jit(solution)/shard_map/reduce_scatter | solution.py:270
  1024.2 13.0 reduce-scatter.39.cloned.1.call-done
  1037.2 16.9 reduce-scatter.47.cloned.1.call-done
  1098.4 14.5 reduce-scatter.85.cloned.1.call-done
  1119.4 54.4 %reduce-scatter.71.cloned.1.call-done = bf16[512,64]{0,1:T(8,128)(2,1)} async-done(((bf16[512,1024]{0,1:T(8,128)(2,1)}), bf16[512,64]{0,1:T(8,128)(2,1)}) %reduce-scatter.71.cloned.1.call-update) | async-done | bytes 65552 | tf_op jit(solution)/shard_map/reduce_scatter | solution.py:56
  1173.8 60.3 %reduce-scatter.69.cloned.1.call-done = bf16[512,64]{0,1:T(8,128)(2,1)} async-done(((bf16[512,1024]{0,1:T(8,128)(2,1)}), bf16[512,64]{0,1:T(8,128)(2,1)}) %reduce-scatter.69.cloned.1.call-update) | async-done | bytes 65552 | tf_op jit(solution)/shard_map/reduce_scatter | solution.py:56
  1235.7 62.8 %reduce-scatter.79.cloned.1.call-done = bf16[1024,64]{0,1:T(8,128)(2,1)} async-done(((bf16[1024,1024]{0,1:T(8,128)(2,1)}), bf16[1024,64]{0,1:T(8,128)(2,1)}) %reduce-scatter.79.cloned.1.call-update) | async-done | bytes 131088 | tf_op jit(solution)/shard_map/reduce_scatter | solution.py:62
  1298.5 64.8 %reduce-scatter.77.cloned.1.call-done = bf16[1024,64]{0,1:T(8,128)(2,1)} async-done(((bf16[1024,1024]{0,1:T(8,128)(2,1)}), bf16[1024,64]{0,1:T(8,128)(2,1)}) %reduce-scatter.77.cloned.1.call-update) | async-done | bytes 131088 | tf_op jit(solution)/shard_map/reduce_scatter | solution.py:62
  1365.0 62.5 %reduce-scatter.75.cloned.1.call-done = bf16[64,1024]{1,0:T(8,128)(2,1)} async-done(((bf16[1024,1024]{1,0:T(8,128)(2,1)}), bf16[64,1024]{1,0:T(8,128)(2,1)}) %reduce-scatter.75.cloned.1.call-update) | async-done | bytes 131088 | tf_op jit(solution)/shard_map/reduce_scatter | solution.py:59
  1427.6 64.8 %reduce-scatter.73.cloned.1.call-done = bf16[64,1024]{1,0:T(8,128)(2,1)} async-done(((bf16[1024,1024]{1,0:T(8,128)(2,1)}), bf16[64,1024]{1,0:T(8,128)(2,1)}) %reduce-scatter.73.cloned.1.call-update) | async-done | bytes 131088 | tf_op jit(solution)/shard_map/reduce_scatter | solution.py:59
  1497.4 55.0 %reduce-scatter.67.cloned.1.call-done = bf16[64,512]{1,0:T(8,128)(2,1)} async-done(((bf16[1024,512]{1,0:T(8,128)(2,1)}), bf16[64,512]{1,0:T(8,128)(2,1)}) %reduce-scatter.67.cloned.1.call-update) | async-done | bytes 65552 | tf_op jit(solution)/shard_map/reduce_scatter | solution.py:53
  1552.4 60.4 %reduce-scatter.65.cloned.1.call-done = bf16[64,512]{1,0:T(8,128)(2,1)} async-done(((bf16[1024,512]{1,0:T(8,128)(2,1)}), bf16[64,512]{1,0:T(8,128)(2,1)}) %reduce-scatter.65.cloned.1.call-update) | async-done | bytes 65552 | tf_op jit(solution)/shard_map/reduce_scatter | solution.py:53
  1614.3 58.4 %reduce-scatter.63.cloned.1.call-done = bf16[64,512]{1,0:T(8,128)(2,1)} async-done(((bf16[1024,512]{1,0:T(8,128)(2,1)}), bf16[64,512]{1,0:T(8,128)(2,1)}) %reduce-scatter.63.cloned.1.call-update) | async-done | bytes 65552 | tf_op jit(solution)/shard_map/reduce_scatter | solution.py:50
  1672.8 60.6 %reduce-scatter.61.cloned.1.call-done = bf16[64,512]{1,0:T(8,128)(2,1)} async-done(((bf16[1024,512]{1,0:T(8,128)(2,1)}), bf16[64,512]{1,0:T(8,128)(2,1)}) %reduce-scatter.61.cloned.1.call-update) | async-done | bytes 65552 | tf_op jit(solution)/shard_map/reduce_scatter | solution.py:50
  1734.9 58.3 %reduce-scatter.59.cloned.1.call-done = bf16[64,512]{1,0:T(8,128)(2,1)} async-done(((bf16[1024,512]{1,0:T(8,128)(2,1)}), bf16[64,512]{1,0:T(8,128)(2,1)}) %reduce-scatter.59.cloned.1.call-update) | async-done | bytes 65552 | tf_op jit(solution)/shard_map/reduce_scatter | solution.py:47
  1793.2 60.4 %reduce-scatter.57.cloned.1.call-done = bf16[64,512]{1,0:T(8,128)(2,1)} async-done(((bf16[1024,512]{1,0:T(8,128)(2,1)}), bf16[64,512]{1,0:T(8,128)(2,1)}) %reduce-scatter.57.cloned.1.call-update) | async-done | bytes 65552 | tf_op jit(solution)/shard_map/reduce_scatter | solution.py:47
  1855.1 86.7 %reduce-scatter.83.cloned.1.call-done = bf16[64,3072]{1,0:T(8,128)(2,1)} async-done(((bf16[1024,3072]{1,0:T(8,128)(2,1)}), bf16[64,3072]{1,0:T(8,128)(2,1)}) %reduce-scatter.83.cloned.1.call-update) | async-done | bytes 393232 | tf_op jit(solution)/shard_map/reduce_scatter | solution.py:65
  1941.8 88.7 %reduce-scatter.81.cloned.1.call-done = bf16[64,3072]{1,0:T(8,128)(2,1)} async-done(((bf16[1024,3072]{1,0:T(8,128)(2,1)}), bf16[64,3072]{1,0:T(8,128)(2,1)}) %reduce-scatter.81.cloned.1.call-update) | async-done | bytes 393232 | tf_op jit(solution)/shard_map/reduce_scatter | solution.py:65
  (541 shorter events, 325.6 us)
Async XLA Ops:
  7.2 67.7 %all-gather.12.cloned.1.call-start = ((), (), s32[]{:S(2)}) async-start(), calls=%async_computation.28 | async-start | bytes 6684672 | tf_op jit(solution)/shard_map/all_gather | solution.py:102
  7.9 105.7 %all-gather.20.cloned.1.call-start = ((), (), s32[]{:S(2)}) async-start(), calls=%async_computation.32 | async-start | bytes 1114112 | tf_op jit(solution)/shard_map/all_gather | solution.py:97
  8.7 144.0 %all-gather.18.cloned.1.call-start = ((), (), s32[]{:S(2)}) async-start(), calls=%async_computation.31 | async-start | bytes 1114112 | tf_op jit(solution)/shard_map/all_gather | solution.py:96
  9.4 182.2 %all-gather.14.cloned.1.call-start = ((), (), s32[]{:S(2)}) async-start(), calls=%async_computation.29 | async-start | bytes 1114112 | tf_op jit(solution)/shard_map/all_gather | solution.py:98
  10.0 233.7 %all-gather.32.cloned.1.call-start = ((), (), s32[]{:S(2)}) async-start(), calls=%async_computation.40 | async-start | bytes 4456448 | tf_op jit(solution)/shard_map/all_gather | solution.py:143
  158.0 137.4 %all-gather.30.cloned.1.call-start = ((), (), s32[]{:S(2)}) async-start(), calls=%async_computation.39 | async-start | bytes 4456448 | tf_op jit(solution)/shard_map/all_gather | solution.py:144
  194.1 139.9 %all-gather.24.cloned.1.call-start = ((), (), s32[]{:S(2)}) async-start(), calls=%async_computation.34 | async-start | bytes 1114112 | tf_op jit(solution)/shard_map/all_gather | solution.py:99
  194.9 156.2 %reduce-scatter.37.cloned.1.call-start = ((), (), s32[]{:S(2)}) async-start(), calls=%async_computation.41 | async-start | bytes 786432 | tf_op jit(solution)/shard_map/reduce_scatter | solution.py:175
  337.0 67.9 %all-gather.26.cloned.1.call-start = ((), (), s32[]{:S(2)}) async-start(), calls=%async_computation.36 | async-start | bytes 2228224 | tf_op jit(solution)/shard_map/all_gather | solution.py:100
  337.7 99.6 %all-gather.28.cloned.1.call-start = ((), (), s32[]{:S(2)}) async-start(), calls=%async_computation.37 | async-start | bytes 2228224 | tf_op jit(solution)/shard_map/all_gather | solution.py:101
  338.3 150.8 %all-gather.22.cloned.1.call-start = ((), (), s32[]{:S(2)}) async-start(), calls=%async_computation.33 | async-start | bytes 4456448 | tf_op jit(solution)/shard_map/all_gather | solution.py:143
  385.7 155.4 %all-gather.16.cloned.1.call-start = ((), (), s32[]{:S(2)}) async-start(), calls=%async_computation.30 | async-start | bytes 4456448 | tf_op jit(solution)/shard_map/all_gather | solution.py:144
  388.0 170.8 %reduce-scatter.49.cloned.1.call-start = ((), (), s32[]{:S(2)}) async-start(), calls=%async_computation.47 | async-start | bytes 786432 | tf_op jit(solution)/shard_map/reduce_scatter | solution.py:223
  442.9 130.9 %reduce-scatter.33.cloned.1.call-start = ((), (), s32[]{:S(2)}) async-start(), calls=%async_computation.35 | async-start | bytes 786432 | tf_op jit(solution)/shard_map/reduce_scatter | solution.py:175
  556.6 130.3 %reduce-scatter.51.cloned.1.call-start = ((), (), s32[]{:S(2)}) async-start(), calls=%async_computation.48 | async-start | bytes 4456448 | tf_op jit(solution)/shard_map/reduce_scatter | solution.py:264
  614.1 148.1 %reduce-scatter.53.cloned.1.call-start = ((), (), s32[]{:S(2)}) async-start(), calls=%async_computation.49 | async-start | bytes 4456448 | tf_op jit(solution)/shard_map/reduce_scatter | solution.py:270
  628.5 153.7 %reduce-scatter.55.cloned.1.call-start = ((), (), s32[]{:S(2)}) async-start(), calls=%async_computation.50 | async-start | bytes 786432 | tf_op jit(solution)/shard_map/reduce_scatter | solution.py:322
  765.8 48.3 %reduce-scatter.41.cloned.1.call-start = ((), (), s32[]{:S(2)}) async-start(), calls=%async_computation.43 | async-start | bytes 786432 | tf_op jit(solution)/shard_map/reduce_scatter | solution.py:223
  800.6 31.0 %reduce-scatter.35.cloned.1.call-start = ((), (), s32[]{:S(2)}) async-start(), calls=%async_computation.38 | async-start | bytes 786432 | tf_op jit(solution)/shard_map/reduce_scatter | solution.py:194
  804.2 140.6 %reduce-scatter.43.cloned.1.call-start = ((), (), s32[]{:S(2)}) async-start(), calls=%async_computation.44 | async-start | bytes 4456448 | tf_op jit(solution)/shard_map/reduce_scatter | solution.py:264
  872.3 148.4 %reduce-scatter.45.cloned.1.call-start = ((), (), s32[]{:S(2)}) async-start(), calls=%async_computation.45 | async-start | bytes 4456448 | tf_op jit(solution)/shard_map/reduce_scatter | solution.py:270
  886.8 150.4 %reduce-scatter.39.cloned.1.call-start = ((), (), s32[]{:S(2)}) async-start(), calls=%async_computation.42 | async-start | bytes 786432 | tf_op jit(solution)/shard_map/reduce_scatter | solution.py:194
  890.2 163.9 %reduce-scatter.47.cloned.1.call-start = ((), (), s32[]{:S(2)}) async-start(), calls=%async_computation.46 | async-start | bytes 786432 | tf_op jit(solution)/shard_map/reduce_scatter | solution.py:322
  1023.9 68.6 %reduce-scatter.87.cloned.1.call-start = ((), (), s32[]{:S(2)}) async-start(), calls=%async_computation.66 | async-start | bytes 2359296
  1058.2 54.7 %reduce-scatter.85.cloned.1.call-start = ((), (), s32[]{:S(2)}) async-start(), calls=%async_computation.65 | async-start | bytes 2359296
  1060.1 113.7 %reduce-scatter.71.cloned.1.call-start = ((), (), s32[]{:S(2)}) async-start(), calls=%async_computation.58 | async-start | bytes 1114112 | tf_op jit(solution)/shard_map/reduce_scatter | solution.py:56
  1063.0 171.2 %reduce-scatter.69.cloned.1.call-start = ((), (), s32[]{:S(2)}) async-start(), calls=%async_computation.57 | async-start | bytes 1114112 | tf_op jit(solution)/shard_map/reduce_scatter | solution.py:56
  1065.9 232.6 %reduce-scatter.79.cloned.1.call-start = ((), (), s32[]{:S(2)}) async-start(), calls=%async_computation.62 | async-start | bytes 2228224 | tf_op jit(solution)/shard_map/reduce_scatter | solution.py:62
  1069.5 293.8 %reduce-scatter.77.cloned.1.call-start = ((), (), s32[]{:S(2)}) async-start(), calls=%async_computation.61 | async-start | bytes 2228224 | tf_op jit(solution)/shard_map/reduce_scatter | solution.py:62
  1073.4 354.1 %reduce-scatter.75.cloned.1.call-start = ((), (), s32[]{:S(2)}) async-start(), calls=%async_computation.60 | async-start | bytes 2228224 | tf_op jit(solution)/shard_map/reduce_scatter | solution.py:59
  1075.7 416.7 %reduce-scatter.73.cloned.1.call-start = ((), (), s32[]{:S(2)}) async-start(), calls=%async_computation.59 | async-start | bytes 2228224 | tf_op jit(solution)/shard_map/reduce_scatter | solution.py:59
  1079.2 473.2 %reduce-scatter.67.cloned.1.call-start = ((), (), s32[]{:S(2)}) async-start(), calls=%async_computation.56 | async-start | bytes 1114112 | tf_op jit(solution)/shard_map/reduce_scatter | solution.py:53
  1080.9 532.0 %reduce-scatter.65.cloned.1.call-start = ((), (), s32[]{:S(2)}) async-start(), calls=%async_computation.55 | async-start | bytes 1114112 | tf_op jit(solution)/shard_map/reduce_scatter | solution.py:53
  1083.4 589.4 %reduce-scatter.63.cloned.1.call-start = ((), (), s32[]{:S(2)}) async-start(), calls=%async_computation.54 | async-start | bytes 1114112 | tf_op jit(solution)/shard_map/reduce_scatter | solution.py:50
  1085.9 647.5 %reduce-scatter.61.cloned.1.call-start = ((), (), s32[]{:S(2)}) async-start(), calls=%async_computation.53 | async-start | bytes 1114112 | tf_op jit(solution)/shard_map/reduce_scatter | solution.py:50
  1088.4 704.8 %reduce-scatter.59.cloned.1.call-start = ((), (), s32[]{:S(2)}) async-start(), calls=%async_computation.52 | async-start | bytes 1114112 | tf_op jit(solution)/shard_map/reduce_scatter | solution.py:47
  1089.9 763.6 %reduce-scatter.57.cloned.1.call-start = ((), (), s32[]{:S(2)}) async-start(), calls=%async_computation.51 | async-start | bytes 1114112 | tf_op jit(solution)/shard_map/reduce_scatter | solution.py:47
  1092.4 849.3 %reduce-scatter.83.cloned.1.call-start = ((), (), s32[]{:S(2)}) async-start(), calls=%async_computation.64 | async-start | bytes 6684672 | tf_op jit(solution)/shard_map/reduce_scatter | solution.py:65
  1098.4 932.1 %reduce-scatter.81.cloned.1.call-start = ((), (), s32[]{:S(2)}) async-start(), calls=%async_computation.63 | async-start | bytes 6684672 | tf_op jit(solution)/shard_map/reduce_scatter | solution.py:65
  1118.6 375.5 %copy-start.35 = (bf16[2,64,1024]{2,1,0:T(8,128)(2,1)S(1)}, bf16[2,64,1024]{2,1,0:T(8,128)(2,1)}, u32[]{:S(2)}) copy-start(bf16[2,64,1024]{2,1,0:T(8,128)(2,1)} %reduce-scatter.47.cloned.1.call-done) | copy-start | bytes 786436
  1118.6 375.5 %copy-start.59 = (f32[2,1024]{1,0:T(2,128)S(1)}, f32[2,1024]{1,0:T(2,128)}, u32[]{:S(2)}) copy-start(f32[2,1024]{1,0:T(2,128)} %copy-done.58) | copy-start | bytes 24580
  1118.6 375.5 %copy-start.69 = (f32[2,64]{1,0:T(2,128)S(1)}, f32[2,64]{1,0:T(2,128)}, u32[]{:S(2)}) copy-start(f32[2,64]{1,0:T(2,128)} %get-tuple-element.89) | copy-start | bytes 1540
  1118.6 375.5 %copy-start.78 = (f32[2,64]{1,0:T(2,128)S(1)}, f32[2,64]{1,0:T(2,128)}, u32[]{:S(2)}) copy-start(f32[2,64]{1,0:T(2,128)} %copy-done.76) | copy-start | bytes 1540
  1118.6 375.5 %copy-start.84 = (f32[2,64]{1,0:T(2,128)S(1)}, f32[2,64]{1,0:T(2,128)}, u32[]{:S(2)}) copy-start(f32[2,64]{1,0:T(2,128)} %copy-done.82) | copy-start | bytes 1540
  1118.6 375.5 %copy-start.91 = (f32[2,64]{1,0:T(2,128)S(1)}, f32[2,64]{1,0:T(2,128)}, u32[]{:S(2)}) copy-start(f32[2,64]{1,0:T(2,128)} %copy-done.89) | copy-start | bytes 1540
  1118.6 375.5 %copy-start.114 = (f32[2,64]{1,0:T(2,128)S(1)}, f32[2,64]{1,0:T(2,128)}, u32[]{:S(2)}) copy-start(f32[2,64]{1,0:T(2,128)} %copy-done.112) | copy-start | bytes 1540
  1118.6 375.5 %copy-start.117 = (f32[2,64]{1,0:T(2,128)S(1)}, f32[2,64]{1,0:T(2,128)}, u32[]{:S(2)}) copy-start(f32[2,64]{1,0:T(2,128)} %copy-done.115) | copy-start | bytes 1540
  1118.6 375.5 %copy-start.120 = (f32[2,64]{1,0:T(2,128)S(1)}, f32[2,64]{1,0:T(2,128)}, u32[]{:S(2)}) copy-start(f32[2,64]{1,0:T(2,128)} %copy-done.118) | copy-start | bytes 1540
  (129 other events, 5497.6 us)
Sparse Core Ops, SparseCore 0:
  10.3 64.5 all-gather.11
  77.0 36.5 all-gather.19
  115.8 36.8 all-gather.17
  154.7 36.8 all-gather.13
  194.2 49.4 all-gather.31
  246.3 49.0 all-gather.29
  297.6 36.4 all-gather.23
  337.1 13.9 reduce-scatter.36
  353.5 41.3 all-gather.25
  397.1 40.1 all-gather.27
  439.7 49.3 all-gather.21
  492.0 49.0 all-gather.15
  544.0 13.0 reduce-scatter.48
  559.1 14.5 reduce-scatter.32
  614.2 72.6 reduce-scatter.50
  690.6 71.5 reduce-scatter.52
  765.9 16.1 reduce-scatter.54
  800.7 13.2 reduce-scatter.40
  817.0 14.5 reduce-scatter.34
  872.4 72.3 reduce-scatter.42
  949.2 71.4 reduce-scatter.44
  1023.5 13.6 reduce-scatter.38
  1039.5 14.5 reduce-scatter.46
  1058.4 26.0 reduce-scatter.86
  1086.8 26.0 reduce-scatter.84
  1116.4 57.4 reduce-scatter.70
  1177.7 56.3 reduce-scatter.68
  1237.9 60.5 reduce-scatter.78
  1302.7 60.5 reduce-scatter.76
  1366.9 60.6 reduce-scatter.74
  1431.8 60.5 reduce-scatter.72
  1496.0 56.3 reduce-scatter.66
  1556.3 56.4 reduce-scatter.64
  1616.4 56.3 reduce-scatter.62
  1676.8 56.4 reduce-scatter.60
  1736.8 56.3 reduce-scatter.58
  1797.1 56.3 reduce-scatter.56
  1857.5 84.2 reduce-scatter.82
  1946.1 84.3 reduce-scatter.80
where the time goes:
time: 2050 us; the launch traced here: 2040 us
  waiting for transfers between devices  1580 us (77%)
  matrix products  176 us (9%)
  local copies, waits for them, and re-layouts  90.2 us (4%)
  blocking collectives  85.6 us (4%)
  other arithmetic  85.1 us (4%)
    reduce_scatter x2, waiting for transfers between devices, reduce_grads(): lax.psum_scatter(gradients[6].astype(jnp.bfloat16), 'seq', scatter_dimens...  175 us
    reduce_scatter x2, waiting for transfers between devices, per_device(): lax.psum_scatter(part_values.reshape(batch_items, frames_total, head_cols...  129 us
    reduce_scatter x2, waiting for transfers between devices, reduce_grads(): lax.psum_scatter(gradients[5].astype(jnp.bfloat16), 'seq', scatter_dimens...  128 us
    reduce_scatter x2, waiting for transfers between devices, reduce_grads(): lax.psum_scatter(gradients[4].astype(jnp.bfloat16), 'seq', scatter_dimens...  127 us
    reduce_scatter x2, waiting for transfers between devices, reduce_grads(): lax.psum_scatter(gradients[1].astype(jnp.bfloat16), 'seq', scatter_dimens...  119 us
    reduce_scatter x2, waiting for transfers between devices, reduce_grads(): lax.psum_scatter(gradients[0].astype(jnp.bfloat16), 'seq', scatter_dimens...  119 us
    reduce_scatter x2, waiting for transfers between devices, reduce_grads(): lax.psum_scatter(gradients[2].astype(jnp.bfloat16), 'seq', scatter_dimens...  115 us
    reduce_scatter x2, waiting for transfers between devices, reduce_grads(): lax.psum_scatter(gradients[3].astype(jnp.bfloat16), 'seq', scatter_dimens...  115 us
  transfers between devices with their start and end apart: 39, of which 36 were waited for; matrix products, arithmetic and copies ran while one was open for 13% of the time, Pallas kernels for 0%

commit v1 on v0

v1 whole, which is shorter than its diff:
```python
from functools import partial
import math

import jax
import jax.numpy as jnp
from jax import lax
from jax.experimental import pallas as pl
from jax.experimental.pallas import tpu as pltpu
from jax.sharding import PartitionSpec as P

D = 1024
HEAD_DIM = 64
EPSILON = 1e-06
NEGATIVE = -1e30
BF = jnp.bfloat16
F32 = jnp.float32
HIGHEST = lax.Precision.HIGHEST
MESH = pl.DeviceIdType.MESH
ANY = pl.BlockSpec(memory_space=pl.ANY)
VMEM = pl.BlockSpec(memory_space=pltpu.VMEM)
LIMIT = 60 * 1024 * 1024


def nn(a, b):
    return lax.dot_general(a, b, (((1,), (0,)), ((), ())), preferred_element_type=F32)


def nt(a, b):
    return lax.dot_general(a, b, (((1,), (1,)), ((), ())), preferred_element_type=F32)


class Place:
    def __init__(self, S, T, I):
        self.S, self.T, self.I = S, T, I
        self.Z, self.R = S // 4, S // I
        self.Q = self.R // 2
        self.s, self.t = lax.axis_index("seq"), lax.axis_index("tp")
        self.z = lax.div(self.s, 4)
        self.x = lax.rem(lax.div(self.s, 2), 2)
        self.c = lax.rem(self.s, 2)
        self.i = lax.div(self.s, self.R)
        self.r = lax.rem(self.s, self.R)
        self.q = lax.div(self.r, 2)

    def at(self, z=None, x=None, c=None, t=None):
        z = self.z if z is None else z
        x = self.x if x is None else x
        c = self.c if c is None else c
        t = self.t if t is None else t
        return ((z * 2 + x) * 2 + c, t)

    def tp(self, k):
        return (self.s, lax.rem(self.t + k, self.T))

    def zs(self, k):
        return lax.rem(self.z + k, self.Z)

    def group(self, k, c=None):
        c = self.c if c is None else c
        return (self.i * self.R + lax.rem(self.q + k, self.Q) * 2 + c, self.t)


class Wires:
    def __init__(self, send, recv, local):
        self.send, self.recv, self.local = send, recv, local
        self.remote_count = self.local_count = 0
        self.sent = []

    def push(self, src, dst, device):
        n = self.remote_count
        self.remote_count += 1
        copy = pltpu.make_async_remote_copy(
            src_ref=src,
            dst_ref=dst,
            send_sem=self.send.at[n],
            recv_sem=self.recv.at[n],
            device_id=device,
            device_id_type=MESH,
        )
        copy.start()
        self.sent.append(copy)
        return copy

    def move(self, src, dst):
        n = self.local_count
        self.local_count += 1
        copy = pltpu.make_async_copy(src, dst, self.local.at[n])
        copy.start()
        return copy

    def close(self):
        for copy in self.sent:
            copy.wait_send()


def landed(copies):
    for copy in copies:
        copy.wait_recv()


def greet_all(place):
    total = place.S * place.T
    me = place.s * place.T + place.t
    barrier = pltpu.get_barrier_semaphore()

    def body(d, carry):
        other = lax.rem(me + d, total)
        pl.semaphore_signal(
            barrier,
            inc=1,
            device_id=(lax.div(other, place.T), lax.rem(other, place.T)),
            device_id_type=MESH,
        )
        return carry

    lax.fori_loop(1, total, body, 0)
    pl.semaphore_wait(barrier, total - 1)


def greet_group(place):
    barrier = pltpu.get_barrier_semaphore()
    pl.semaphore_signal(barrier, inc=1, device_id=place.group(0, 1 - place.c), device_id_type=MESH)
    for k in range(1, place.Q):
        pl.semaphore_signal(barrier, inc=1, device_id=place.group(k), device_id_type=MESH)
    pl.semaphore_wait(barrier, place.Q)


def scatter_rows(place, send, recv, copy_of):
    total = place.S * place.T
    me = place.s * place.T + place.t

    def copy(d):
        other = lax.rem(me + d, total)
        s, t = lax.div(other, place.T), lax.rem(other, place.T)
        src, dst = copy_of(s, t)
        return pltpu.make_async_remote_copy(
            src_ref=src,
            dst_ref=dst,
            send_sem=send.at[d],
            recv_sem=recv.at[d],
            device_id=(s, t),
            device_id_type=MESH,
        )

    def start(d, carry):
        copy(d).start()
        return carry

    def wait(d, carry):
        copy(d).wait()
        return carry

    lax.fori_loop(1, total, start, 0)
    return lambda: lax.fori_loop(1, total, wait, 0)


class Gather:
    def __init__(self, place, wires, src, dst):
        self.p, self.w, self.src, self.dst = place, wires, src, dst
        half = src.shape[0] // 2
        self.upper, self.lower = pl.ds(0, half), pl.ds(half, half)

    def phase0(self):
        p, w, dst = self.p, self.w, self.dst
        own = dst.at[0, p.z, p.x, p.c]
        self.own = w.move(self.src, own)
        self.along = [w.push(self.src, own, p.at(z=p.zs(k))) for k in range(1, p.Z)]

    def phase1(self):
        p, w, dst = self.p, self.w, self.dst
        self.own.wait()
        landed(self.along)
        line = dst.at[0, :, p.x, p.c]
        self.sides = [
            w.push(
                dst.at[0, :, p.x, p.c, self.upper],
                dst.at[0, :, p.x, p.c, self.upper],
                p.at(x=1 - p.x),
            )
        ]
        for k in range(1, p.T):
            self.sides.append(
                w.push(
                    dst.at[0, :, p.x, p.c, self.lower],
                    dst.at[p.T - k, :, p.x, p.c, self.lower],
                    p.tp(k),
                )
            )
        self.cores = [w.push(line, line, p.at(c=1 - p.c))]

    def phase2(self):
        p, w, dst = self.p, self.w, self.dst
        landed(self.sides)
        self.last = []
        for k in range(1, p.T):
            self.last.append(
                w.push(
                    dst.at[0, :, :, p.c, self.upper],
                    dst.at[p.T - k, :, :, p.c, self.upper],
                    p.tp(k),
                )
            )
        part = dst.at[:, :, p.x, p.c, self.lower]
        self.last.append(w.push(part, part, p.at(x=1 - p.x)))
        part = dst.at[0, :, 1 - p.x, p.c, self.upper]
        self.cores.append(w.push(part, part, p.at(c=1 - p.c)))
        part = dst.at[pl.ds(1, p.T - 1), :, p.x, p.c, self.lower]
        self.cores.append(w.push(part, part, p.at(c=1 - p.c)))

    def phase3(self):
        p, w, dst = self.p, self.w, self.dst
        landed(self.last)
        part = dst.at[pl.ds(1, p.T - 1), :, :, p.c, self.upper]
        self.cores.append(w.push(part, part, p.at(c=1 - p.c)))
        part = dst.at[:, :, 1 - p.x, p.c, self.lower]
        self.cores.append(w.push(part, part, p.at(c=1 - p.c)))

    def phase4(self):
        landed(self.cores)


class Reduce:
    def __init__(self, place, wires, src, out, own, core, y_up, x_low, x_up, y_low, z_in):
        self.p, self.w, self.src, self.out = place, wires, src, out
        self.own, self.core, self.y_up, self.x_low = own, core, y_up, x_low
        self.x_up, self.y_low, self.z_in = x_up, y_low, z_in
        half = own.shape[3] // 2
        self.half = half
        self.upper, self.lower = pl.ds(0, half), pl.ds(half, half)

    @staticmethod
    def scratch(T, Z, rs, C):
        half = rs // 2
        return [
            pltpu.VMEM((T, Z, 2, rs, C), BF),
            pltpu.VMEM((T, Z, 2, rs, C), BF),
            pltpu.VMEM((T - 1, Z, 2, half, C), BF),
            pltpu.VMEM((T, Z, half, C), BF),
            pltpu.VMEM((Z, half, C), BF),
            pltpu.VMEM((T - 1, Z, half, C), BF),
            pltpu.VMEM((Z - 1, rs, C), BF),
        ]

    def phase0(self):
        p, w, src = self.p, self.w, self.src
        self.mine = w.move(src.at[:, :, :, p.c], self.own)
        self.pair = [w.push(src.at[:, :, :, 1 - p.c], self.core, p.at(c=1 - p.c))]

    def phase1(self):
        p, w, own = self.p, self.w, self.own
        self.mine.wait()
        landed(self.pair)

        def add(n, carry):
            k, z = lax.div(n, p.Z), lax.rem(n, p.Z)
            for x in range(2):
                own[k, z, x] = own[k, z, x] + self.core[k, z, x]
            return carry

        lax.fori_loop(0, p.T * p.Z, add, 0)
        self.sides = [
            w.push(own.at[k, :, :, self.upper], self.y_up.at[k - 1], p.tp(k))
            for k in range(1, p.T)
        ]
        self.sides.append(w.push(own.at[:, :, 1 - p.x, self.lower], self.x_low, p.at(x=1 - p.x)))

    def phase2(self):
        p, w, own = self.p, self.w, self.own
        landed(self.sides)

        def add(z, carry):
            for x in range(2):
                total = own[0, z, x, self.upper].astype(F32)
                for k in range(1, p.T):
                    total = total + self.y_up[k - 1, z, x].astype(F32)
                own[0, z, x, self.upper] = total.astype(BF)
            for k in range(p.T):
                own[k, z, p.x, self.lower] = own[k, z, p.x, self.lower] + self.x_low[k, z]
            return carry

        lax.fori_loop(0, p.Z, add, 0)
        self.last = [w.push(own.at[0, :, 1 - p.x, self.upper], self.x_up, p.at(x=1 - p.x))]
        for k in range(1, p.T):
            self.last.append(
                w.push(own.at[k, :, p.x, self.lower], self.y_low.at[k - 1], p.tp(k))
            )

    def phase3(self):
        p, w, own = self.p, self.w, self.own
        landed(self.last)

        def add(z, carry):
            own[0, z, p.x, self.upper] = own[0, z, p.x, self.upper] + self.x_up[z]
            total = own[0, z, p.x, self.lower].astype(F32)
            for k in range(1, p.T):
                total = total + self.y_low[k - 1, z].astype(F32)
            own[0, z, p.x, self.lower] = total.astype(BF)
            return carry

        lax.fori_loop(0, p.Z, add, 0)
        self.along = [
            w.push(own.at[0, p.zs(k), p.x], self.z_in.at[k - 1], p.at(z=p.zs(k)))
            for k in range(1, p.Z)
        ]

    def phase4(self):
        p = self.p
        landed(self.along)
        total = self.own[0, p.z, p.x].astype(F32)
        for k in range(1, p.Z):
            total = total + self.z_in[k - 1].astype(F32)
        self.out[...] = total


def swap_items(place, wires, src, dst):
    p = place
    own = wires.move(src.at[p.i], dst.at[p.i])
    copies = []
    for k in range(1, p.I):
        other = lax.rem(p.i + k, p.I)
        copies.append(wires.push(src.at[other], dst.at[p.i], (other * p.R + p.r, p.t)))
    return own, copies


def first_kernel(
    S, T, I, frames, cotangent, parts, w_a, w_f,
    frames_out, cotangent_out, parts_out, all_a, all_f,
    send, recv, local, row_send, row_recv,
):
    p = Place(S, T, I)
    wires = Wires(send, recv, local)
    greet_all(p)
    frames_own, frames_in = swap_items(p, wires, frames, frames_out)
    rows_done = scatter_rows(
        p, row_send, row_recv,
        lambda s, t: (parts.at[t, lax.div(s, p.R)], parts_out.at[p.t, p.s]),
    )
    parts_own = wires.move(parts.at[p.t, p.i], parts_out.at[p.t, p.s])
    a, f = Gather(p, wires, w_a, all_a), Gather(p, wires, w_f, all_f)
    a.phase0()
    cotangent_own, cotangent_in = swap_items(p, wires, cotangent, cotangent_out)
    f.phase0()
    a.phase1()
    f.phase1()
    a.phase2()
    f.phase2()
    a.phase3()
    f.phase3()
    a.phase4()
    f.phase4()
    for own in (frames_own, parts_own, cotangent_own):
        own.wait()
    landed(frames_in)
    landed(cotangent_in)
    rows_done()
    wires.close()


def first_call(S, T, I, frames, cotangent, parts, w_a, w_f):
    rs = w_a.shape[0]
    Z = S // 4
    remote = 2 * (I - 1) + 2 * (Z - 1 + 2 * T + 5)
    out_shape = (
        jax.ShapeDtypeStruct(frames.shape, BF),
        jax.ShapeDtypeStruct(cotangent.shape, BF),
        jax.ShapeDtypeStruct((T, S) + parts.shape[2:], F32),
        jax.ShapeDtypeStruct((T, Z, 2, 2, rs, w_a.shape[1]), BF),
        jax.ShapeDtypeStruct((T, Z, 2, 2, rs, w_f.shape[1]), BF),
    )
    return pl.pallas_call(
        partial(first_kernel, S, T, I),
        out_shape=out_shape,
        in_specs=[ANY] * 5,
        out_specs=(ANY,) * 5,
        scratch_shapes=[
            pltpu.SemaphoreType.DMA((remote,)),
            pltpu.SemaphoreType.DMA((remote,)),
            pltpu.SemaphoreType.DMA((8,)),
            pltpu.SemaphoreType.DMA((S * T,)),
            pltpu.SemaphoreType.DMA((S * T,)),
        ],
        compiler_params=pltpu.CompilerParams(
            collective_id=0, has_side_effects=True, vmem_limit_bytes=LIMIT
        ),
        name="spread_inputs",
    )(frames, cotangent, parts, w_a, w_f)


def share_kernel(S, T, I, own, out, send, recv, local):
    p = Place(S, T, I)
    wires = Wires(send, recv, local)
    greet_group(p)
    across = [wires.push(own, out.at[p.Q - k, 0], p.group(k)) for k in range(1, p.Q)]
    sibling = p.group(0, 1 - p.c)
    cores = [wires.push(own, out.at[0, 1], sibling)]
    mine = wires.move(own, out.at[0, 0])
    for k in range(1, p.Q):
        across[k - 1].wait_recv()
        cores.append(wires.push(out.at[p.Q - k, 0], out.at[p.Q - k, 1], sibling))
    landed(cores)
    mine.wait()
    wires.close()


def share_call(S, T, I, own):
    Q = S // I // 2
    count = 2 * Q
    return pl.pallas_call(
        partial(share_kernel, S, T, I),
        out_shape=jax.ShapeDtypeStruct((Q, 2) + own.shape, BF),
        in_specs=[ANY],
        out_specs=ANY,
        scratch_shapes=[
            pltpu.SemaphoreType.DMA((count,)),
            pltpu.SemaphoreType.DMA((count,)),
            pltpu.SemaphoreType.DMA((1,)),
        ],
        compiler_params=pltpu.CompilerParams(
            collective_id=1, has_side_effects=True, vmem_limit_bytes=LIMIT
        ),
        name="share_rows",
    )(own)


def unshare_kernel(S, T, I, parts, out, near, far, pair, send, recv, local):
    p = Place(S, T, I)
    wires = Wires(send, recv, local)
    greet_group(p)
    core = wires.push(parts.at[:, 1], near, p.group(0, 1 - p.c))
    core.wait_recv()
    across = []
    for k in range(1, p.Q):
        pair[k - 1] = parts[k, 0] + near[k]
        across.append(wires.push(pair.at[k - 1], far.at[k - 1], p.group(k)))
    total = parts[0, 0].astype(F32) + near[0].astype(F32)
    for k in range(1, p.Q):
        across[k - 1].wait_recv()
        total = total + far[k - 1].astype(F32)
    out[...] = total
    wires.close()


def unshare_call(S, T, I, parts):
    Q = S // I // 2
    block = parts.shape[2:]
    return pl.pallas_call(
        partial(unshare_kernel, S, T, I),
        out_shape=jax.ShapeDtypeStruct(block, F32),
        in_specs=[VMEM],
        out_specs=VMEM,
        scratch_shapes=[
            pltpu.VMEM((Q,) + block, BF),
            pltpu.VMEM((Q - 1,) + block, BF),
            pltpu.VMEM((Q - 1,) + block, BF),
            pltpu.SemaphoreType.DMA((Q,)),
            pltpu.SemaphoreType.DMA((Q,)),
            pltpu.SemaphoreType.DMA((1,)),
        ],
        compiler_params=pltpu.CompilerParams(
            collective_id=2, has_side_effects=True, vmem_limit_bytes=LIMIT
        ),
        name="sum_rows",
    )(parts)


def last_kernel(S, T, I, *refs):
    (layer, grads, rows, grad_a, grad_f,
     layer_out, grads_out, rows_out, sum_a, sum_f) = refs[:10]
    scratch_a, scratch_f = refs[10:17], refs[17:24]
    send, recv, local, row_send, row_recv = refs[24:]
    p = Place(S, T, I)
    wires = Wires(send, recv, local)
    greet_all(p)
    f = Reduce(p, wires, grad_f, sum_f, *scratch_f)
    a = Reduce(p, wires, grad_a, sum_a, *scratch_a)
    f.phase0()
    a.phase0()
    grads_own, grads_in = swap_items(p, wires, grads, grads_out)
    layer_own, layer_in = swap_items(p, wires, layer, layer_out)
    rows_done = scatter_rows(
        p, row_send, row_recv, lambda s, t: (rows.at[t], rows_out.at[p.t, p.s])
    )
    rows_own = wires.move(rows.at[p.t], rows_out.at[p.t, p.s])
    f.phase1()
    a.phase1()
    f.phase2()
    a.phase2()
    f.phase3()
    a.phase3()
    f.phase4()
    a.phase4()
    for own in (grads_own, layer_own, rows_own):
        own.wait()
    landed(grads_in)
    landed(layer_in)
    rows_done()
    wires.close()


def last_call(S, T, I, layer, grads, rows, grad_a, grad_f):
    Z, rs = S // 4, grad_a.shape[4]
    ca, cf = grad_a.shape[5], grad_f.shape[5]
    remote = 2 * (I - 1) + 2 * (Z + 2 * T + 2)
    return pl.pallas_call(
        partial(last_kernel, S, T, I),
        out_shape=(
            jax.ShapeDtypeStruct(layer.shape, BF),
            jax.ShapeDtypeStruct(grads.shape, BF),
            jax.ShapeDtypeStruct((T, S) + rows.shape[1:], F32),
            jax.ShapeDtypeStruct((rs, ca), F32),
            jax.ShapeDtypeStruct((rs, cf), F32),
        ),
        in_specs=[ANY] * 5,
        out_specs=(ANY, ANY, ANY, VMEM, VMEM),
        scratch_shapes=Reduce.scratch(T, Z, rs, ca)
        + Reduce.scratch(T, Z, rs, cf)
        + [
            pltpu.SemaphoreType.DMA((remote,)),
            pltpu.SemaphoreType.DMA((remote,)),
            pltpu.SemaphoreType.DMA((8,)),
            pltpu.SemaphoreType.DMA((S * T,)),
            pltpu.SemaphoreType.DMA((S * T,)),
        ],
        compiler_params=pltpu.CompilerParams(
            collective_id=3, has_side_effects=True, vmem_limit_bytes=LIMIT
        ),
        name="collect_outputs",
    )(layer, grads, rows, grad_a, grad_f)


def swap_pairs(v):
    lane = lax.broadcasted_iota(jnp.int32, v.shape, 1)
    return jnp.where(lax.rem(lane, 2) == 0, pltpu.roll(v, 127, 1), pltpu.roll(v, 1, 1))


def head_split(v):
    lane = lax.broadcasted_iota(jnp.int32, v.shape, 1)
    zero = jnp.zeros_like(v)
    return jnp.where(lane < HEAD_DIM, v, zero), jnp.where(lane < HEAD_DIM, zero, v)


def first_lane(rows):
    lane = lax.broadcasted_iota(jnp.int32, (rows, 128), 1)
    return jnp.where(lane == 0, 1.0, 0.0).astype(BF)


def attend_kernel(
    rows, cb, xm_ref, w_ref, cos_ref, sin_ref, mask_ref,
    q_ref, k_ref, v_ref, att_ref, lse_ref, branch_ref,
):
    step = pl.program_id(0)
    q_lin = nn(xm_ref[0:rows, :], w_ref[0, :, 0:cb])
    k_lin = nn(xm_ref[...], w_ref[0, :, cb : 2 * cb])
    v_ref[...] = nn(xm_ref[...], w_ref[0, :, 2 * cb : 3 * cb]).astype(BF)
    ones = first_lane(rows)
    factor = HEAD_DIM**-0.5
    for p in range(cb // 128):
        lanes = slice(p * 128, p * 128 + 128)
        q2, k2 = q_lin[:, lanes], k_lin[:, lanes]
        q2 = (q2 * cos_ref[0:rows, :] + swap_pairs(q2) * sin_ref[0:rows, :]).astype(BF)
        q2 = q2 * jnp.asarray(factor, BF)
        k2 = (k2 * cos_ref[...] + swap_pairs(k2) * sin_ref[...]).astype(BF)
        q_ref[:, lanes] = q2
        k_ref[:, lanes] = k2
        k_long = jnp.concatenate([k2, mask_ref[...]], axis=1)
        v_turned = v_ref[:, lanes].T
        outs = []
        for h, q1 in enumerate(head_split(q2)):
            scores = nt(k_long, jnp.concatenate([q1, ones], axis=1))
            highest = jnp.max(scores, axis=0, keepdims=True)
            unnormed = jnp.exp(scores - highest)
            total = jnp.sum(unnormed, axis=0, keepdims=True)
            probs = (unnormed * (1.0 / total)).astype(BF)
            lse_ref[0, pl.ds(2 * p + h, 1), :] = highest + jnp.log(total)
            outs.append(nn(v_turned[h * HEAD_DIM : (h + 1) * HEAD_DIM], probs))
        att_ref[:, lanes] = jnp.concatenate(outs, axis=0).T.astype(BF)
    part = nt(att_ref[...], w_ref[0, :, 3 * cb : 4 * cb])

    @pl.when(step == 0)
    def _():
        branch_ref[...] = part

    @pl.when(step > 0)
    def _():
        branch_ref[...] += part


def attend_call(rows, cb, xm, w_all, cosine, sine, mask):
    T, _, wide = w_all.shape
    per_t = wide // (4 * cb)
    L = xm.shape[0]
    steps = T * per_t
    fixed = lambda n: (0, 0)
    column = lambda n: (0, n)
    return pl.pallas_call(
        partial(attend_kernel, rows, cb),
        grid=(steps,),
        out_shape=(
            jax.ShapeDtypeStruct((rows, D), BF),
            jax.ShapeDtypeStruct((L, D), BF),
            jax.ShapeDtypeStruct((L, D), BF),
            jax.ShapeDtypeStruct((rows, D), BF),
            jax.ShapeDtypeStruct((steps, 8, rows), F32),
            jax.ShapeDtypeStruct((rows, D), F32),
        ),
        in_specs=[
            pl.BlockSpec((L, D), fixed),
            pl.BlockSpec((1, D, 4 * cb), lambda n: (n // per_t, 0, n % per_t)),
            pl.BlockSpec((L, 128), fixed),
            pl.BlockSpec((L, 128), fixed),
            pl.BlockSpec((L, 128), fixed),
        ],
        out_specs=(
            pl.BlockSpec((rows, cb), column),
            pl.BlockSpec((L, cb), column),
            pl.BlockSpec((L, cb), column),
            pl.BlockSpec((rows, cb), column),
            pl.BlockSpec((1, 8, rows), lambda n: (n, 0, 0)),
            pl.BlockSpec((rows, D), fixed),
        ),
        compiler_params=pltpu.CompilerParams(vmem_limit_bytes=LIMIT),
        name="attend",
    )(xm, w_all, cosine, sine, mask)


def attend_back_kernel(
    rows, cb, db_ref, xm_ref, w_ref, cos_ref, sin_ref, mask_ref,
    q_ref, k_ref, v_ref, att_ref, lse_ref,
    grad_ref, dx_ref, xm_turned, db_turned, dx_sum,
):
    step = pl.program_id(0)

    @pl.when(step == 0)
    def _():
        xm_turned[...] = xm_ref[...].T
        db_turned[...] = db_ref[...].T
        dx_sum[...] = jnp.zeros_like(dx_sum)

    d_att = nn(db_ref[...], w_ref[0, :, 3 * cb : 4 * cb]).astype(BF)
    grad_ref[0, :, 3 * cb : 4 * cb] = nn(db_turned[...], att_ref[...]).astype(BF)
    ones = first_lane(rows)
    factor = HEAD_DIM**-0.5
    dqs, dks, dvs = [], [], []
    for p in range(cb // 128):
        lanes = slice(p * 128, p * 128 + 128)
        q2, k2, v2 = q_ref[:, lanes], k_ref[:, lanes], v_ref[:, lanes]
        k_long = jnp.concatenate([k2, mask_ref[...]], axis=1)
        k_turned = k2.T
        dq_parts, ds_all, p_all = [], [], []
        q_heads, d_heads = head_split(q2), head_split(d_att[:, lanes])
        for h in range(2):
            scores = nt(k_long, jnp.concatenate([q_heads[h], ones], axis=1))
            probs = jnp.exp(scores - lse_ref[0, pl.ds(2 * p + h, 1), :])
            d_probs = nt(v2, d_heads[h])
            row_dot = jnp.sum(probs * d_probs, axis=0, keepdims=True)
            d_scores = (probs * (d_probs - row_dot)).astype(BF)
            dq_parts.append(nn(k_turned[h * HEAD_DIM : (h + 1) * HEAD_DIM], d_scores))
            ds_all.append(d_scores)
            p_all.append(probs.astype(BF))
        dk2 = nn(jnp.concatenate(ds_all, axis=1), jnp.concatenate(q_heads, axis=0))
        dv2 = nn(jnp.concatenate(p_all, axis=1), jnp.concatenate(d_heads, axis=0))
        dq2 = jnp.concatenate(dq_parts, axis=0).T * factor
        dqs.append(
            (dq2 * cos_ref[0:rows, :] - swap_pairs(dq2) * sin_ref[0:rows, :]).astype(BF)
        )
        dks.append((dk2 * cos_ref[...] - swap_pairs(dk2) * sin_ref[...]).astype(BF))
        dvs.append(dv2.astype(BF))
    dq, dk, dv = (jnp.concatenate(v, axis=1) for v in (dqs, dks, dvs))
    grad_ref[0, :, 0:cb] = nn(xm_turned[:, 0:rows], dq).astype(BF)
    grad_ref[0, :, cb : 2 * cb] = nn(xm_turned[...], dk).astype(BF)
    grad_ref[0, :, 2 * cb : 3 * cb] = nn(xm_turned[...], dv).astype(BF)
    dx_sum[...] += nt(
        jnp.concatenate([dk, dv], axis=1), w_ref[0, :, cb : 3 * cb]
    )
    dx_sum[0:rows, :] += nt(dq, w_ref[0, :, 0:cb])

    @pl.when(step == pl.num_programs(0) - 1)
    def _():
        dx_ref[...] = dx_sum[...].astype(BF)


def attend_back_call(rows, cb, d_branch, xm, w_all, cosine, sine, mask, q, k, v, att, lse):
    T, _, wide = w_all.shape
    per_t = wide // (4 * cb)
    L = xm.shape[0]
    steps = T * per_t
    fixed = lambda n: (0, 0)
    column = lambda n: (0, n)
    weight = pl.BlockSpec((1, D, 4 * cb), lambda n: (n // per_t, 0, n % per_t))
    return pl.pallas_call(
        partial(attend_back_kernel, rows, cb),
        grid=(steps,),
        out_shape=(
            jax.ShapeDtypeStruct(w_all.shape, BF),
            jax.ShapeDtypeStruct((L, D), BF),
        ),
        in_specs=[
            pl.BlockSpec((rows, D), fixed),
            pl.BlockSpec((L, D), fixed),
            weight,
            pl.BlockSpec((L, 128), fixed),
            pl.BlockSpec((L, 128), fixed),
            pl.BlockSpec((L, 128), fixed),
            pl.BlockSpec((rows, cb), column),
            pl.BlockSpec((L, cb), column),
            pl.BlockSpec((L, cb), column),
            pl.BlockSpec((rows, cb), column),
            pl.BlockSpec((1, 8, rows), lambda n: (n, 0, 0)),
        ],
        out_specs=(weight, pl.BlockSpec((L, D), fixed)),
        scratch_shapes=[
            pltpu.VMEM((D, L), BF),
            pltpu.VMEM((D, rows), BF),
            pltpu.VMEM((L, D), F32),
        ],
        compiler_params=pltpu.CompilerParams(vmem_limit_bytes=LIMIT),
        name="attend_back",
    )(d_branch, xm, w_all, cosine, sine, mask, q, k, v, att, lse)


def layer_stats(values):
    center = values - jnp.mean(values, axis=-1, keepdims=True)
    inverse = lax.rsqrt(jnp.mean(center * center, axis=-1, keepdims=True) + EPSILON)
    return center * inverse, inverse


def layer_back(normed, inverse, incoming):
    return inverse * (
        incoming
        - jnp.mean(incoming, axis=-1, keepdims=True)
        - normed * jnp.mean(incoming * normed, axis=-1, keepdims=True)
    )


def feed_kernel(
    hb, frames_ref, cot_ref, branch_ref, live_ref, mod_ref, w_ref,
    layer_ref, grad_ref, dmid_ref, dbranch_ref, dmod_ref,
    mf_ref, mf_turned, db_ref, db_turned, mid_ref, normed_ref, out_sum, dmf_sum,
):
    step = pl.program_id(0)
    gate_attn, shift_ff = mod_ref[2:3, :], mod_ref[3:4, :]
    scale_ff, gate_ff = mod_ref[4:5, :], mod_ref[5:6, :]

    @pl.when(step == 0)
    def _():
        middle = frames_ref[...].astype(F32) + gate_attn * live_ref[...] * branch_ref[...]
        mid_ref[...] = middle
        normed, _ = layer_stats(middle)
        low = normed.astype(BF)
        normed_ref[...] = low
        modulated = (low.astype(F32) * (1.0 + scale_ff) + shift_ff).astype(BF)
        mf_ref[...] = modulated
        mf_turned[...] = modulated.T
        d_branch = (cot_ref[...].astype(F32) * gate_ff).astype(BF)
        db_ref[...] = d_branch
        db_turned[...] = d_branch.T
        out_sum[...] = jnp.zeros_like(out_sum)
        dmf_sum[...] = jnp.zeros_like(dmf_sum)

    w_up, w_down = w_ref[0, :, 0:hb], w_ref[0, :, hb : 2 * hb]
    upper = nn(mf_ref[...], w_up)
    square = upper * upper
    slope = 0.7978845608
    tanh = jnp.tanh(slope * (upper + 0.044715 * upper * square))
    half = 0.5 * (1.0 + tanh)
    active = (upper * half).astype(BF)
    bend = half + 0.5 * upper * (1.0 - tanh * tanh) * (slope * (1.0 + 3 * 0.044715 * square))
    out_sum[...] += nt(active, w_down)
    d_upper = (nn(db_ref[...], w_down) * bend).astype(BF)
    dmf_sum[...] += nt(d_upper, w_up)
    grad_ref[0, :, 0:hb] = nn(mf_turned[...], d_upper).astype(BF)
    grad_ref[0, :, hb : 2 * hb] = nn(db_turned[...], active).astype(BF)

    @pl.when(step == pl.num_programs(0) - 1)
    def _():
        middle, branch_f = mid_ref[...], out_sum[...]
        layer_ref[...] = (middle + gate_ff * branch_f).astype(BF)
        cot = cot_ref[...].astype(F32)
        normed, inverse = layer_stats(middle)
        dmf = dmf_sum[...]
        d_mid = cot + layer_back(normed, inverse, dmf * (1.0 + scale_ff))
        dmid_ref[...] = d_mid
        live = d_mid * live_ref[...]
        dbranch_ref[...] = (live * gate_attn).astype(BF)
        dmod_ref[...] = jnp.zeros_like(dmod_ref)
        dmod_ref[0:1, :] = jnp.sum(live * branch_ref[...], axis=0, keepdims=True)
        dmod_ref[1:2, :] = jnp.sum(dmf, axis=0, keepdims=True)
        dmod_ref[2:3, :] = jnp.sum(dmf * normed_ref[...].astype(F32), axis=0, keepdims=True)
        dmod_ref[3:4, :] = jnp.sum(cot * branch_f, axis=0, keepdims=True)


def feed_call(hb, frames, cotangent, branch, live, mod, w_all):
    T, _, wide = w_all.shape
    per_t = wide // (2 * hb)
    rows = frames.shape[0]
    fixed = lambda n: (0, 0)
    weight = pl.BlockSpec((1, D, 2 * hb), lambda n: (n // per_t, 0, n % per_t))
    row_block = pl.BlockSpec((rows, D), fixed)
    return pl.pallas_call(
        partial(feed_kernel, hb),
        grid=(T * per_t,),
        out_shape=(
            jax.ShapeDtypeStruct((rows, D), BF),
            jax.ShapeDtypeStruct(w_all.shape, BF),
            jax.ShapeDtypeStruct((rows, D), F32),
            jax.ShapeDtypeStruct((rows, D), BF),
            jax.ShapeDtypeStruct((8, D), F32),
        ),
        in_specs=[
            row_block, row_block, row_block,
            pl.BlockSpec((rows, 1), fixed), pl.BlockSpec((6, D), fixed), weight,
        ],
        out_specs=(row_block, weight, row_block, row_block, pl.BlockSpec((8, D), fixed)),
        scratch_shapes=[
            pltpu.VMEM((rows, D), BF),
            pltpu.VMEM((D, rows), BF),
            pltpu.VMEM((rows, D), BF),
            pltpu.VMEM((D, rows), BF),
            pltpu.VMEM((rows, D), F32),
            pltpu.VMEM((rows, D), BF),
            pltpu.VMEM((rows, D), F32),
            pltpu.VMEM((rows, D), F32),
        ],
        compiler_params=pltpu.CompilerParams(vmem_limit_bytes=LIMIT),
        name="feed_forward",
    )(frames, cotangent, branch, live, mod, w_all)


def pack(blocks, width):
    rows = blocks[0].shape[0]
    cut = [b.reshape(rows, -1, 1, width) for b in blocks]
    return jnp.concatenate(cut, axis=2).reshape(rows, -1)


def unpack(packed, count, width):
    cut = packed.reshape(packed.shape[0], -1, count, width)
    return [cut[:, :, n].reshape(packed.shape[0], -1) for n in range(count)]


def per_device(
    S, T, frames, time_embed, lengths, w_query, w_key, w_value, w_out, w_up, w_down, w_mod, out_grad
):
    micro, rows_own, fl, _ = frames.shape
    batch = lengths.shape[1]
    I = micro * rows_own
    R = S // I
    Q = R // 2
    rs = w_query.shape[0]
    rows = I * fl
    L = R * rows
    cb = min(256, w_query.shape[1])
    hb = min(512, w_up.shape[1])
    s, t = lax.axis_index("seq"), lax.axis_index("tp")
    item = s // R
    place_r = s % R

    w_a = pack([w_query, w_key, w_value, w_out.T], cb)
    w_f = pack([w_up, w_down.T], hb)
    silu = jax.nn.silu(time_embed).astype(BF).reshape(micro * batch, D)
    silu_own = lax.dynamic_slice_in_dim(silu, s * rs, rs, 1)
    cols = w_mod.shape[1]
    parts = jnp.dot(silu_own, w_mod, preferred_element_type=F32)
    parts = parts.reshape(micro, T, rows_own, cols // 128, 128)
    parts = parts.transpose(1, 0, 2, 3, 4).reshape(T, I, cols // 128, 128)
    frames_in, cot_in, parts_in, all_a, all_f = first_call(
        S, T, I, frames.reshape(I, fl, D), out_grad.reshape(I, fl, D), parts, w_a, w_f
    )
    mod = jnp.sum(parts_in, axis=1).astype(BF).astype(F32).reshape(6, D)
    all_a = all_a.reshape(T, D, w_a.shape[1])
    all_f = all_f.reshape(T, D, w_f.shape[1])
    frame_rows = frames_in.reshape(rows, D)
    cot_rows = cot_in.reshape(rows, D)

    g = jnp.arange(R)
    r_of = (place_r // 2 + g // 2) % Q * 2 + (place_r % 2 + g % 2) % 2
    pos = fl * (jnp.arange(I)[None, :] * R + r_of[:, None])
    pos = (pos[:, :, None] + jnp.arange(fl)).reshape(L)
    length = lengths[item // rows_own, t * rows_own + item % rows_own]
    alive = pos < length
    live = alive[:rows].astype(F32)[:, None]
    lane = jnp.arange(128)
    mask = jnp.where((lane[None, :] == 0) & ~alive[:, None], NEGATIVE, 0.0).astype(BF)
    column = (lane % HEAD_DIM // 2).astype(F32)
    inverse = jnp.exp(column * (-2.0 * math.log(10000.0) / HEAD_DIM))
    angles = pos.astype(F32)[:, None] * inverse[None, :]
    cosine = jnp.cos(angles)
    sine = jnp.sin(angles) * jnp.where(lane % 2 == 0, -1.0, 1.0)

    normed_a, inverse_a = layer_stats(frame_rows.astype(F32))
    normed_low = normed_a.astype(BF).astype(F32)
    xm_own = (normed_low * (1.0 + mod[1:2]) + mod[0:1]).astype(BF)
    xm = share_call(S, T, I, xm_own).reshape(L, D)
    q, k, v, att, lse, branch = attend_call(rows, cb, xm, all_a, cosine, sine, mask)
    layer, grad_f, d_mid, d_branch, d_rows = feed_call(
        hb, frame_rows, cot_rows, branch, live, mod, all_f
    )
    grad_a, dx = attend_back_call(
        rows, cb, d_branch, xm, all_a, cosine, sine, mask, q, k, v, att, lse
    )
    d_mod_a = unshare_call(S, T, I, dx.reshape(Q, 2, rows, D))
    grad_in = d_mid + layer_back(normed_a, inverse_a, d_mod_a * (1.0 + mod[1:2]))
    d_modulation = jnp.concatenate(
        [
            jnp.sum(d_mod_a, axis=0, keepdims=True),
            jnp.sum(d_mod_a * normed_low, axis=0, keepdims=True),
            d_rows[0:4],
        ],
        axis=0,
    ).reshape(T, cols // 128, 128)
    shape6 = (T, S // 4, 2, 2, rs)
    layer_out, grad_input, mod_in, sum_a, sum_f = last_call(
        S, T, I, layer.reshape(I, fl, D), grad_in.astype(BF).reshape(I, fl, D), d_modulation,
        grad_a.reshape(shape6 + (w_a.shape[1],)), grad_f.reshape(shape6 + (w_f.shape[1],)),
    )
    mod_items = jnp.sum(mod_in.reshape(T, I, R, cols), axis=2).reshape(T * I, cols)
    silu_items = silu.reshape(micro, T, rows_own, D).transpose(1, 0, 2, 3).reshape(T * I, D)
    silu_items = lax.dynamic_slice_in_dim(silu_items, s * rs, rs, 1).astype(F32)
    grad_mod = jnp.dot(silu_items.T, mod_items, precision=HIGHEST)
    g_query, g_key, g_value, g_out = unpack(sum_a, 4, cb)
    g_up, g_down = unpack(sum_f, 2, hb)
    return (
        layer_out.reshape(frames.shape),
        grad_input.reshape(frames.shape),
        g_query,
        g_key,
        g_value,
        g_out.T,
        g_up,
        g_down.T,
        grad_mod,
    )


def solution(mesh):
    S, T = mesh.shape["seq"], mesh.shape["tp"]
    rows = P(None, "tp", "seq", None)
    return jax.shard_map(
        partial(per_device, S, T),
        mesh=mesh,
        in_specs=(
            rows,
            P(),
            P(),
            P("seq", "tp"),
            P("seq", "tp"),
            P("seq", "tp"),
            P("tp", "seq"),
            P("seq", "tp"),
            P("tp", "seq"),
            P("seq", "tp"),
            rows,
        ),
        out_specs=(
            rows,
            rows,
            P("seq", "tp"),
            P("seq", "tp"),
            P("seq", "tp"),
            P("tp", "seq"),
            P("seq", "tp"),
            P("tp", "seq"),
            P("seq", "tp"),
        ),
        check_vma=False,
    )
```

time: 2050 us -> 419 us (0.20)
  waiting for transfers between devices: 1580 us -> 0 us
  Pallas kernels: 0 us -> 371 us
  matrix products: 176 us -> 1.69 us
  blocking collectives: 85.6 us -> 0 us
  other arithmetic: 85.1 us -> 17 us
  local copies, waits for them, and re-layouts: 90.2 us -> 24.3 us
    reduce_scatter x26 -> x0, waiting for transfers between devices: 1190 us -> none  [the longest x2 175 us: reduce_grads(): lax.psum_scatter(gradients[6].astype(jnp.bfloat16), 'seq', scatter_dimens...]
    pallas_call x0 -> x7, Pallas kernels: none -> 371 us  [the longest x1 143 us: first_call(): pl.pallas_call(partial(first_kernel, S, T, I), out_shape=out_shape, in_sp...]
    all_gather x11 -> x0, waiting for transfers between devices: 368 us -> none  [the longest x2 93.9 us: per_device(): lax.all_gather(key_rows, 'seq', axis=1, tiled=True)]
    dot_general x52 -> x2, matrix products: 176 us -> 1.69 us  [the longest x1 1.46 us: per_device(): grad_mod = jnp.dot(silu_items.T, mod_items, precision=HIGHEST)]
    all_gather x10 -> x0, blocking collectives: 85.6 us -> none  [the longest x2 23 us: per_device(): branch_f_all = lax.all_gather(delta_branch_f, 'tp', axis=0, tiled=True)]
    convert_element_type x6 -> x2, local copies, waits for them, and re-layouts: 27.6 us -> 0.12 us  [the longest x1 0.08 us: per_device(): angles = pos.astype(F32)[:, None] * inverse[None, :]]
    all_gather x4 -> x0, local copies, waits for them, and re-layouts: 25.1 us -> none  [the longest x2 12.6 us: per_device(): lax.all_gather(key_rows, 'seq', axis=1, tiled=True)]
  transfers between devices with their start and end apart: 39 -> 0, of which waited for: 36 -> 0; matrix products, arithmetic and copies ran while one was open for 13% -> 0% of each run, Pallas kernels for 0% -> 0%
where the time goes in v1:
time: 419 us; the launch traced here: 415 us
  Pallas kernels  371 us (89%)
  local copies, waits for them, and re-layouts  24.3 us (6%)
  other arithmetic  17 us (4%)
    pallas_call x1, Pallas kernels, first_call(): pl.pallas_call(partial(first_kernel, S, T, I), out_shape=out_shape, in_sp...  143 us
    pallas_call x1, Pallas kernels, last_call(): pl.pallas_call(partial(last_kernel, S, T, I), out_shape=(jax.ShapeDtypeSt...  121 us
    pallas_call x1, Pallas kernels, attend_back_call(): pl.pallas_call(partial(attend_back_kernel, rows, cb), grid=(steps,), out_...  34 us
    pallas_call x1, Pallas kernels, attend_call(): pl.pallas_call(partial(attend_kernel, rows, cb), grid=(steps,), out_shape...  20.2 us
    pallas_call x1, Pallas kernels, unshare_call(): pl.pallas_call(partial(unshare_kernel, S, T, I), out_shape=jax.ShapeDtype...  19.6 us
    pallas_call x1, Pallas kernels, share_call(): pl.pallas_call(partial(share_kernel, S, T, I), out_shape=jax.ShapeDtypeSt...  18.5 us
    pallas_call x1, Pallas kernels, feed_call(): pl.pallas_call(partial(feed_kernel, hb), grid=(T * per_t,), out_shape=(ja...  15 us

profile of v1, /device:TPU:0, one launch (start us, length us, event | category | flops | bytes accessed | tf_op | source)
XLA Modules:
  0.0 414.9 jit_solution(10508371974703094663)
XLA Ops:
  0.7 1.3 dynamic_slice.10
  2.2 0.7 fusion.21
  2.9 0.1 not.12
  3.1 0.8 fusion.7
  4.0 0.2 convolution_bitcast_fusion
  4.3 0.6 copy.27
  4.9 0.8 reshape.347.live_ref
  5.7 0.9 reshape.341
  6.6 0.9 reshape.342
  7.5 0.9 reshape.343
  8.3 0.9 reshape.344
  9.2 0.6 pad_maximum_fusion
  9.9 0.9 reshape.317.w_a
  10.7 0.9 select_convert_fusion.mask_ref
  11.6 1.0 reshape.345
  12.6 1.0 reshape.346
  13.6 0.6 pad_maximum_fusion.1
  14.3 0.9 reshape.320.w_f
  15.1 3.0 fusion.6
  18.2 142.5 %spread_inputs.1 = (bf16[4,64,1024]{2,1,0:T(8,128)(2,1)}, bf16[4,64,1024]{2,1,0:T(8,128)(2,1)}, f32[2,16,24,128]{3,2,1,0:T(8,128)}, bf16[2,4,2,2,64,2048]{5,4,3,...) custom-call(bf16[4,64,1024]{2,1,0:T(8,128)(2,1)} %bitcast.70, bf16[4,64,1024]{2,1,0:T(8,128)(2,1)} %bitcast.71, ...), custom_call_target="tpu_custom_call" | custom-call | tf_op jit(solution)/shard_map/spread_inputs/pallas_call | solution.py:370
  160.7 1.2 convert_reduce_fusion
  162.0 1.3 fusion.1
  163.4 1.0 reduce_sum.74
  164.5 2.1 fusion.3.own
  166.6 18.5 %share_rows.1 = bf16[2,2,256,1024]{3,2,1,0:T(8,128)(2,1)} custom-call(bf16[256,1024]{1,0:T(8,128)(2,1)} %fusion.3.own), custom_call_target="tpu_custom_call" | custom-call | tf_op jit(solution)/shard_map/share_rows/pallas_call | solution.py:408
  185.2 20.2 %attend.1 = (bf16[256,1024]{1,0:T(8,128)(2,1)}, bf16[1024,1024]{1,0:T(8,128)(2,1)}, bf16[1024,1024]{1,0:T(8,128)(2,1)}, bf16[256,1024]{1,0:T(8,128)(2,1)}, f32[4,8,256]{2,1,0:T(8,128)}, /*index=5*/f32[256,1024]{1,0:T(8,128)}) custom-call(bf16[1024,1024]{1,0:T(8,128)(2,1)} %bitcast.60, bf16[2,1024,2048]{2,1,0:T(8,128)(2,1)} %bitcast.58, ...), custom_call_target="tpu_custom_call" | custom-call | tf_op jit(solution)/shard_map/attend/pallas_call | solution.py:595
  205.4 15.0 %feed_forward.1 = (bf16[256,1024]{1,0:T(8,128)(2,1)}, bf16[2,1024,2048]{2,1,0:T(8,128)(2,1)}, f32[256,1024]{1,0:T(8,128)}, bf16[256,1024]{1,0:T(8,128)(2,1)}, f32[8,1024]{1,0:T(8,128)}) custom-call(bf16[256,1024]{1,0:T(8,128)(2,1)} %bitcast.62, bf16[256,1024]{1,0:T(8,128)(2,1)} %bitcast.79, f32[256,1024]{1,0:T(8,128)} %get-tuple-element.36.branch_ref, ...), custom_call_target="tpu_custom_call" | custom-call | tf_op jit(solution)/shard_map/feed_forward/pallas_call | solution.py:799
  220.4 34.0 %attend_back.1 = (bf16[2,1024,2048]{2,1,0:T(8,128)(2,1)}, bf16[1024,1024]{1,0:T(8,128)(2,1)}) custom-call(bf16[256,1024]{1,0:T(8,128)(2,1)} %get-tuple-element.40.db_ref, bf16[1024,1024]{1,0:T(8,128)(2,1)} %bitcast.61, bf16[2,1024,2048]{2,1,0:T(8,128)(2,1)} %bitcast.59, f32[1024,128]{1,0:T(8,128)} %get-tuple-element.70.cos_ref, ...), custom_call_target="tpu_custom_call" | custom-call | tf_op jit(solution)/shard_map/attend_back/pallas_call | solution.py:690
  254.4 19.6 %sum_rows.1 = f32[256,1024]{1,0:T(8,128)} custom-call(bf16[2,2,256,1024]{3,2,1,0:T(8,128)(2,1)} %bitcast.66), custom_call_target="tpu_custom_call" | custom-call | tf_op jit(solution)/shard_map/sum_rows/pallas_call | solution.py:446
  274.0 1.8 fusion.4
  275.8 2.4 add_convert_fusion
  278.3 0.6 reshape.329.refs_2_
  278.9 121.1 %collect_outputs.1 = (bf16[4,64,1024]{2,1,0:T(8,128)(2,1)}, bf16[4,64,1024]{2,1,0:T(8,128)(2,1)}, f32[2,16,24,128]{3,2,1,0:T(8,128)}, f32[64,2048]{1,0:T(8,128)}, f32[64,2048]{1,0:T(8,128)}) custom-call(bf16[4,64,1024]{2,1,0:T(8,128)(2,1)} %bitcast.72, bf16[4,64,1024]{2,1,0:T(8,128)(2,1)} %bitcast.67, f32[2,24,128]{2,1,0:T(8,128)} %reshape.329.refs_2_, ...), custom_call_target="tpu_custom_call" | custom-call | tf_op jit(solution)/shard_map/collect_outputs/pallas_call | solution.py:504
  400.0 1.2 reshape.337
  401.3 0.2 reduce_sum.79
  401.5 1.4 reshape.334
  402.9 1.7 slice_reduce_fusion.2
  404.6 0.7 copy.40
  405.3 0.7 copy.39
  406.0 0.7 copy.38
  406.6 0.7 copy.37
  407.3 1.5 reshape.335
  408.8 1.6 slice_reduce_fusion
  410.4 0.8 copy.42
  411.1 0.8 copy.41
  411.9 1.5 fusion.10
  413.4 0.8 copy.47
  414.2 0.8 copy.48
  (37 shorter events, 0.7 us)
Async XLA Ops:
  0.6 3.4 copy-start
  164.5 40.9 %copy-start.5 = (f32[6,1024]{1,0:T(8,128)}, f32[6,1024]{1,0:T(8,128)S(1)}, u32[]{:S(2)}) copy-start(f32[6,1024]{1,0:T(8,128)S(1)} %reshape.339.mod_ref) | copy-start | bytes 73732
  220.4 53.6 %copy-start.1 = (bf16[4,64,1024]{2,1,0:T(8,128)(2,1)S(1)}, bf16[4,64,1024]{2,1,0:T(8,128)(2,1)}, u32[]{:S(2)}) copy-start(bf16[4,64,1024]{2,1,0:T(8,128)(2,1)} %get-tuple-element.32) | copy-start | bytes 1572868
  220.4 55.4 %copy-start.2 = (f32[256,1024]{1,0:T(8,128)S(1)}, f32[256,1024]{1,0:T(8,128)}, u32[]{:S(2)}) copy-start(f32[256,1024]{1,0:T(8,128)} %get-tuple-element.39) | copy-start | bytes 3145732
  220.4 57.8 %copy-start.6 = (f32[8,1024]{1,0:T(8,128)S(1)}, f32[8,1024]{1,0:T(8,128)}, u32[]{:S(2)}) copy-start(f32[8,1024]{1,0:T(8,128)} %get-tuple-element.47) | copy-start | bytes 98308
  400.0 13.3 %copy-start.4 = (bf16[4,64,1024]{2,1,0:T(8,128)(2,1)S(1)}, bf16[4,64,1024]{2,1,0:T(8,128)(2,1)}, u32[]{:S(2)}) copy-start(bf16[4,64,1024]{2,1,0:T(8,128)(2,1)} %get-tuple-element.50) | copy-start | bytes 1572868
  400.0 14.1 %copy-start.3 = (bf16[4,64,1024]{2,1,0:T(8,128)(2,1)S(1)}, bf16[4,64,1024]{2,1,0:T(8,128)(2,1)}, u32[]{:S(2)}) copy-start(bf16[4,64,1024]{2,1,0:T(8,128)(2,1)} %get-tuple-element.51) | copy-start | bytes 1572868
